TPU v7x, 32 devices: a whole 2x2x4 slice. The times are simulated.
32 devices in a mesh: groups: 1, expert: 8 (over z, y), dp: 4 (over x, core).
Axes of the slice: x: 2, y: 2, z: 4, core: 2. Of those that a mesh axis runs over, the one named last changes fastest.
Arguments:
- queries: bfloat16 [2048, 4096], P(('groups', 'dp'), 'expert'), may hold values from -6 to 6
- keys_in: bfloat16 [2048, 4096], P(('groups', 'dp'), 'expert'), may hold values from -6 to 6
- values_in: bfloat16 [2048, 4096], P(('groups', 'dp'), 'expert'), may hold values from -6 to 6
- gate_in: bfloat16 [2048, 4096], P(('groups', 'dp'), 'expert'), may hold values from -6 to 6
- beta: float32 [2048, 32], P(('groups', 'dp'), 'expert'), may hold values from 0.1 to 1
- decay: float32 [2048, 32], P(('groups', 'dp'), 'expert'), may hold values from -1 to 0
- lengths: int32 [4, 4], P(('groups', 'dp')), may hold values from 1 to 256, 512 in all within a row
- cache: float32 [16, 32, 128, 128], P(('groups', 'dp'), 'expert'), may hold values from -6 to 6
- norm_gain: float32 [128], replicated, may hold values from 0.1 to 1.9
- out_proj: bfloat16 [4096, 2048], P('expert'), may hold values from -0.09375 to 0.09375
- residual: bfloat16 [2048, 2048], P(('groups', 'dp', 'expert')), may hold values from -6 to 6
- post_gain: float32 [2048], replicated, may hold values from 0.1 to 1.9
- expert_ids: int32 [2048, 10], P(('groups', 'dp', 'expert')), may hold values from 0 to 31, all different within a row; in each aligned block of 64 rows (0 to 63, 64 to 127, ...) at most 25 rows name the same one
- route_weights: float32 [2048, 10], P(('groups', 'dp', 'expert')), may hold values from 0.05 to 1
- gate_up: bfloat16 [32, 2048, 512], P(('expert', 'dp')), may hold values from -0.125 to 0.125
- down_proj: bfloat16 [32, 256, 2048], P(('expert', 'dp')), may hold values from -0.375 to 0.375
Outputs:
- moe_out: bfloat16 [2048, 2048], P(('groups', 'dp', 'expert'))
- attn_out: bfloat16 [2048, 2048], P(('groups', 'dp', 'expert'))
- new_states: float32 [16, 32, 128, 128], P(('groups', 'dp'), 'expert')
Inputs may be any that keep to these rules, and one draw needn't show every extreme that they name: Each row of lengths fills its shard's 512 rows; the longest span of each row is exactly 256. `expert_ids`: each row names 10 different experts. Within the 64 rows of one device no expert is named more than 25 times, a bound that some block reaches; every expert is named somewhere.
All inputs are finite; a program needn't handle non-finite values.
Results may differ from a plain program's by a relative error of at most 0.025.
Values may be sent and summed in bfloat16 or wider, within the bound.
A program may use at most 64 MiB of HBM per device.

v0:
```python
import jax
import jax.numpy as jnp
from jax import lax
from jax.sharding import PartitionSpec as P

HIGH = lax.Precision.HIGHEST
epsilon = 1e-06
block_rows = 64


def unit_rows(values):
    return values * lax.rsqrt(jnp.sum(values * values, axis=-1, keepdims=True) + epsilon)


def block_step(states, item):
    query_b, key_b, value_b, beta_b, decay_b, member_b = item
    size = query_b.shape[0]
    places = jnp.arange(size)
    shared = jnp.dot(member_b, member_b.T, precision=HIGH) > 0.5
    inside = shared & (places[:, None] >= places[None, :])
    strict_part = inside & (places[:, None] > places[None, :])
    running = jnp.dot(inside.astype(jnp.float32), decay_b, precision=HIGH).T
    log_gaps = running[:, :, None] - running[:, None, :]
    decays = jnp.where(inside[None], jnp.exp(jnp.minimum(log_gaps, 0.0)), 0.0)
    key_h = jnp.swapaxes(key_b, 0, 1)
    query_h = jnp.swapaxes(query_b, 0, 1)
    value_h = jnp.swapaxes(value_b, 0, 1)
    beta_h = beta_b.T
    key_dots = jnp.einsum("hik,hjk->hij", key_h, key_h, precision=HIGH)
    strict_terms = jnp.where(strict_part[None], decays * key_dots * beta_h[:, :, None], 0.0)
    identity = jnp.eye(size, dtype=jnp.float32)[None]
    inverse = identity - strict_terms
    powered = strict_terms
    covered = 2
    while covered < size:
        powered = jnp.einsum("hij,hjk->hik", powered, powered, precision=HIGH)
        inverse = jnp.einsum("hij,hjk->hik", inverse, identity + powered, precision=HIGH)
        covered = covered * 2
    growth = jnp.exp(running)
    targets = jnp.concatenate(
        [key_h * (beta_h * growth)[:, :, None], value_h * beta_h[:, :, None]], axis=2
    )
    solved = jnp.einsum("hij,hjc->hic", inverse, targets, precision=HIGH)
    width = key_h.shape[2]
    key_mix = solved[:, :, :width]
    value_mix = solved[:, :, width:]
    recalled = jnp.einsum("hck,hrkv->hrcv", key_mix, states, precision=HIGH)
    recalled = jnp.einsum("cr,hrcv->hcv", member_b, recalled, precision=HIGH)
    updates = value_mix - recalled
    from_state = jnp.einsum("hck,hrkv->hrcv", query_h, states, precision=HIGH)
    from_state = jnp.einsum("cr,hrcv->hcv", member_b, from_state, precision=HIGH)
    query_dots = jnp.einsum("hik,hjk->hij", query_h, key_h, precision=HIGH)
    mixed = growth[:, :, None] * from_state + jnp.einsum(
        "hij,hjv->hiv", query_dots * decays, updates, precision=HIGH
    )
    span_total = jnp.einsum("cr,ch->hr", member_b, decay_b, precision=HIGH)
    end_gaps = span_total[:, :, None] - running[:, None, :]
    carried = jnp.where(member_b.T[None] > 0.5, jnp.exp(jnp.minimum(end_gaps, 0.0)), 0.0)
    fresh = jnp.einsum("hrc,hck,hcv->hrkv", carried, key_h, updates, precision=HIGH)
    states = jnp.exp(span_total)[:, :, None, None] * states + fresh
    return (states, jnp.swapaxes(mixed, 0, 1))


def on_device(
    queries,
    keys_in,
    values_in,
    gate_in,
    beta,
    decay,
    lengths,
    cache,
    norm_gain,
    out_proj,
    residual,
    post_gain,
    expert_ids,
    route_weights,
    gate_up,
    down_proj,
):
    tok_count = queries.shape[0]
    heads = beta.shape[1]
    head_dim = norm_gain.shape[0]
    requests = lengths.shape[1]
    block = min(block_rows, tok_count)
    blocks = tok_count // block
    layout = (blocks, block, heads, head_dim)
    query_n = unit_rows(queries.astype(jnp.float32).reshape(layout)) * head_dim ** (-0.5)
    key_n = unit_rows(keys_in.astype(jnp.float32).reshape(layout))
    value_f = values_in.astype(jnp.float32).reshape(layout)
    ends = jnp.cumsum(lengths[0])
    places = jnp.arange(tok_count, dtype=jnp.int32)
    request = jnp.sum((places[:, None] >= ends[None, :]).astype(jnp.int32), axis=1)
    member = (request[:, None] == jnp.arange(requests, dtype=jnp.int32)[None, :]).astype(
        jnp.float32
    )
    inputs = (
        query_n,
        key_n,
        value_f,
        beta.reshape(blocks, block, heads),
        decay.reshape(blocks, block, heads),
        member.reshape(blocks, block, requests),
    )
    states, mixed = lax.scan(block_step, jnp.swapaxes(cache, 0, 1), inputs)
    new_states = jnp.swapaxes(states, 0, 1)
    mixed = mixed.reshape(tok_count, heads, head_dim)
    gate_f = gate_in.astype(jnp.float32).reshape(tok_count, heads, head_dim)
    scale = lax.rsqrt(jnp.mean(mixed * mixed, axis=-1, keepdims=True) + epsilon)
    normed = (
        (mixed * scale * norm_gain * jax.nn.silu(gate_f))
        .astype(jnp.bfloat16)
        .reshape(tok_count, heads * head_dim)
    )
    tok_local = residual.shape[0]
    attn = lax.psum_scatter(
        jnp.dot(normed, out_proj, preferred_element_type=jnp.float32).astype(jnp.bfloat16),
        "expert",
        scatter_dimension=0,
        tiled=True,
    ).astype(jnp.float32)
    attn_out = (residual.astype(jnp.float32) + attn).astype(jnp.bfloat16)
    stream = attn_out.astype(jnp.float32)
    routed = (
        stream * lax.rsqrt(jnp.mean(stream * stream, axis=-1, keepdims=True) + epsilon) * post_gain
    ).astype(jnp.bfloat16)
    expert_axis = lax.axis_size("expert")
    data_axis = lax.axis_size("dp")
    experts_all = expert_axis * data_axis
    top = expert_ids.shape[1]
    capacity = min(tok_local, max(2, 5 * tok_local * top // (4 * experts_all)))
    slots = experts_all * capacity
    width = routed.shape[1]
    flat_ids = expert_ids.reshape(-1)
    chosen = (flat_ids[:, None] == jnp.arange(experts_all, dtype=jnp.int32)[None, :]).astype(
        jnp.int32
    )
    rank = jnp.sum(chosen * (jnp.cumsum(chosen, axis=0) - 1), axis=1)
    slot_of = flat_ids * capacity + rank
    picks = (slot_of[None, :] == jnp.arange(slots, dtype=jnp.int32)[:, None]).reshape(
        slots, tok_local, top
    )
    picks = jnp.any(picks, axis=2).astype(jnp.bfloat16)
    outgoing = jnp.dot(picks, routed, preferred_element_type=jnp.float32).astype(jnp.bfloat16)
    outgoing = outgoing.reshape(expert_axis, data_axis, capacity, width)
    arrived = lax.all_to_all(
        lax.all_to_all(outgoing, "expert", split_axis=0, concat_axis=0, tiled=True),
        "dp",
        split_axis=1,
        concat_axis=1,
        tiled=True,
    )
    shape = arrived.shape
    flat = arrived.reshape(-1, shape[-1])
    both = jnp.dot(flat, gate_up[0], preferred_element_type=jnp.float32)
    hidden_width = down_proj.shape[1]
    hidden = (jax.nn.silu(both[:, :hidden_width]) * both[:, hidden_width:]).astype(jnp.bfloat16)
    result = jnp.dot(hidden, down_proj[0], preferred_element_type=jnp.float32).astype(jnp.bfloat16)
    returned = lax.all_to_all(
        lax.all_to_all(result.reshape(shape), "expert", split_axis=0, concat_axis=0, tiled=True),
        "dp",
        split_axis=1,
        concat_axis=1,
        tiled=True,
    )
    gathered = jnp.take(returned.reshape(slots, width), slot_of, axis=0).reshape(
        tok_local, top, width
    )
    moe_out = jnp.sum(gathered.astype(jnp.float32) * route_weights[:, :, None], axis=1).astype(
        jnp.bfloat16
    )
    return (moe_out, attn_out, new_states)


def solution(mesh):
    return jax.shard_map(
        on_device,
        mesh=mesh,
        in_specs=(
            P(("groups", "dp"), "expert"),
            P(("groups", "dp"), "expert"),
            P(("groups", "dp"), "expert"),
            P(("groups", "dp"), "expert"),
            P(("groups", "dp"), "expert"),
            P(("groups", "dp"), "expert"),
            P(("groups", "dp"), None),
            P(("groups", "dp"), "expert", None, None),
            P(),
            P("expert", None),
            P(("groups", "dp", "expert"), None),
            P(),
            P(("groups", "dp", "expert"), None),
            P(("groups", "dp", "expert"), None),
            P(("expert", "dp"), None, None),
            P(("expert", "dp"), None, None),
        ),
        out_specs=(
            P(("groups", "dp", "expert"), None),
            P(("groups", "dp", "expert"), None),
            P(("groups", "dp"), "expert", None, None),
        ),
        check_vma=False,
    )
```

profile of v0, /device:TPU:0, one launch (start us, length us, event | category | flops | bytes accessed | tf_op | source)
XLA Modules:
  0.0 527.6 jit_solution(2639585679003318834)
XLA Ops:
  21.4 111.9 %while.12 = (s32[]{:T(128)}, f32[4,4,128,128]{3,2,1,0:T(8,128)S(1)}, f32[8,64,4,128]{3,1,2,0:T(8,128)}, f32[8,64,4]{1,0,2:T(8,128)S(1)}, f32[8,64,4]{1,2,0:T(4,1...) while((s32[]{:T(128)}, ...), condition=%wide.region_9.10_spmd, body=%wide.region_8.9_spmd.sunk | while | flops 860401152 | bytes 12359501 | solution.py:106
  134.9 2.9 copy.143
  138.6 4.1 convolution_convert_fusion.2
  145.6 67.9 %reduce-scatter.2.cloned.1.call-done = bf16[64,2048]{1,0:T(8,128)(2,1)} async-done(((bf16[512,2048]{1,0:T(8,128)(2,1)}), bf16[64,2048]{1,0:T(8,128)(2,1)}) %reduce-scatter.2.cloned.1.call-update) | async-done | bytes 262160 | tf_op jit(solution)/shard_map/reduce_scatter | solution.py:117
  214.8 2.8 convolution_convert_fusion.1
  217.6 4.9 reshape.237
  222.5 4.8 copy.146
  227.3 76.2 %all_to_all.20 = bf16[8,4,25,2048]{3,1,2,0:T(4,128)(2,1)S(1)} all-to-all(bf16[8,4,25,2048]{3,1,2,0:T(4,128)(2,1)S(1)} %copy.146), channel_id=1, replica_groups=mesh['groups'=1,'expert'=8,'dp'=4] {'expert'}, dimensions={0} | all-to-all | bytes 6553600 | tf_op jit(solution)/shard_map/all_to_all | solution.py:148
  305.3 41.1 %all_to_all.21 = bf16[8,4,25,2048]{3,0,2,1:T(8,128)(2,1)S(1)} all-to-all(bf16[8,4,25,2048]{3,0,2,1:T(8,128)(2,1)S(1)} %copy.147), channel_id=1, replica_groups=mesh['groups'=1,'expert'=8,'dp'=4] {'dp'}, dimensions={1} | all-to-all | bytes 6553600 | tf_op jit(solution)/shard_map/all_to_all | solution.py:147
  346.3 3.8 copy.148
  350.2 5.1 reshape.238
  355.2 3.9 fusion.46
  359.1 2.8 convolution_convert_fusion
  361.9 4.9 reshape.239
  366.8 4.8 copy.149
  371.6 76.5 %all_to_all.22 = bf16[8,4,25,2048]{3,1,2,0:T(4,128)(2,1)S(1)} all-to-all(bf16[8,4,25,2048]{3,1,2,0:T(4,128)(2,1)S(1)} %copy.149), channel_id=1, replica_groups=mesh['groups'=1,'expert'=8,'dp'=4] {'expert'}, dimensions={0} | all-to-all | bytes 6553600 | tf_op jit(solution)/shard_map/all_to_all | solution.py:161
  448.1 3.5 copy.150
  451.6 5.1 all-to-all-start.3
  458.0 37.1 %all-to-all-done.3 = bf16[8,4,25,2048]{3,0,2,1:T(8,128)(2,1)} async-done(((bf16[8,4,25,2048]{3,0,2,1:T(8,128)(2,1)}), bf16[8,4,25,2048]{3,0,2,1:T(8,128)(2,1)}, u32[]{:S(2)}, u32[]{:S(2)}) %all-to-all-start.3) | async-done | bytes 3276832 | tf_op jit(solution)/shard_map/all_to_all | solution.py:160
  495.1 5.8 %copy.151 = bf16[8,4,25,2048]{3,2,1,0:T(8,128)(2,1)} copy(bf16[8,4,25,2048]{3,0,2,1:T(8,128)(2,1)} %all-to-all-done.3) | data formatting | bytes 6553600 | tf_op jit(solution)/shard_map/all_to_all | solution.py:160
  500.8 3.4 reshape.240
  504.3 4.1 gather_fusion
  508.4 5.5 %gather.7 = bf16[64,10,2048]{2,1,0:T(8,128)(2,1)} reshape(bf16[640,2048]{1,0:T(8,128)(2,1)} %gather_fusion) | data formatting | bytes 5242880 | tf_op jit(solution)/shard_map/jit(_take)/gather | solution.py:167
  513.9 6.4 %multiply_reduce_fusion = bf16[64,2048]{1,0:T(8,128)(2,1)} fusion(f32[64,10]{1,0:T(8,128)S(1)} %copy.152, bf16[64,10,2048]{2,1,0:T(8,128)(2,1)} %gather.7, pred[64,10]{1,0:T(8,128)(4,1)S(1)} %get-tuple-element.125), kind=kLoop, calls=%fused_computation.74 | loop fusion | flops 5111808 | bytes 2886784 | tf_op jit(solution)/shard_map/reduce_sum | solution.py:170
  (339 shorter events, 133.6 us)
Async XLA Ops:
  7.2 131.4 %copy-start = (bf16[512,2048]{1,0:T(8,128)(2,1)S(1)}, bf16[512,2048]{1,0:T(8,128)(2,1)}, u32[]{:S(2)}) copy-start(bf16[512,2048]{1,0:T(8,128)(2,1)} %param.27) | copy-start | bytes 6291460
  7.2 206.3 %reduce-scatter.2.cloned.1.call-start = ((), (), s32[]{:S(2)}) async-start(), calls=%async_computation.5 | async-start | bytes 2359296 | tf_op jit(solution)/shard_map/reduce_scatter | solution.py:117
  21.4 116.4 %copy-start.6 = (f32[128]{0:T(128)S(1)}, f32[128]{0:T(128)}, u32[]{:S(2)}) copy-start(f32[128]{0:T(128)} %param.26) | copy-start | bytes 1540
  138.6 4.2 copy-start.4
  142.7 72.1 %copy-start.3 = (f32[2048]{0:T(1024)S(1)}, f32[2048]{0:T(1024)}, u32[]{:S(2)}) copy-start(f32[2048]{0:T(1024)} %param.29) | copy-start | bytes 24580
  214.7 7.7 %copy-start.2 = (bf16[64,2048]{1,0:T(8,128)(2,1)}, bf16[64,2048]{1,0:T(8,128)(2,1)S(1)}, u32[]{:S(2)}) copy-start(bf16[64,2048]{1,0:T(8,128)(2,1)S(1)} %get-tuple-element.128) | copy-start | bytes 786436
  350.2 5.1 copy-start.7
  355.2 3.9 copy-start.8
  451.6 5.2 copy-start.5
  451.6 43.4 %all-to-all-start.3 = ((bf16[8,4,25,2048]{3,0,2,1:T(8,128)(2,1)}), bf16[8,4,25,2048]{3,0,2,1:T(8,128)(2,1)}, u32[]{:S(2)}, u32[]{:S(2)}) async-start(bf16[8,4,25,2048]{3,0,2,1:T(8,128)(2,1)} %copy.150), calls=%async_computation.4 | async-start | bytes 6553600 | tf_op jit(solution)/shard_map/all_to_all | solution.py:160
  508.4 12.0 %copy-start.1 = (bf16[512,2048]{1,0:T(8,128)(2,1)S(1)}, bf16[512,2048]{1,0:T(8,128)(2,1)}, u32[]{:S(2)}) copy-start(bf16[512,2048]{1,0:T(8,128)(2,1)} %param.27) | copy-start | bytes 6291460
Sparse Core Ops, SparseCore 0:
  142.8 70.6 reduce-scatter.1
where the time goes:
time: 538 us; the launch traced here: 528 us
  blocking collectives  194 us (36%)
  matrix products  105 us (20%)
  waiting for transfers between devices  105 us (20%)
  local copies, waits for them, and re-layouts  83.1 us (15%)
  other arithmetic  19.3 us (4%)
  between operations  14.8 us (3%)
    all_to_all x1, blocking collectives, on_device(): lax.all_to_all(result.reshape(shape), 'expert', split_axis=0, concat_axis...  76.5 us
    all_to_all x1, blocking collectives, on_device(): lax.all_to_all(outgoing, 'expert', split_axis=0, concat_axis=0, tiled=True)  76.2 us
    reduce_scatter x1, waiting for transfers between devices, on_device(): lax.psum_scatter(jnp.dot(normed, out_proj, preferred_element_type=jnp.flo...  67.9 us
    all_to_all x1, blocking collectives, on_device(): lax.all_to_all(lax.all_to_all(outgoing, 'expert', split_axis=0, concat_ax...  41.1 us
    all_to_all x1, waiting for transfers between devices, on_device(): lax.all_to_all(lax.all_to_all(result.reshape(shape), 'expert', split_axis...  37.1 us
    dot_general x8, matrix products, block_step(): jnp.einsum('hrc,hck,hcv->hrkv', carried, key_h, updates, precision=HIGH)  18.2 us
    dynamic_slice x32, local copies, waits for them, and re-layouts, on_device(): states, mixed = lax.scan(block_step, jnp.swapaxes(cache, 0, 1), inputs)  15.5 us
    dot_general x8, matrix products, block_step(): jnp.einsum('cr,hrcv->hcv', member_b, from_state, precision=HIGH)  10.8 us
  transfers between devices with their start and end apart: 2, of which 2 were waited for; matrix products, arithmetic and copies ran while one was open for 1% of the time, Pallas kernels for 0%

commit v1 on v0

--- a/solution.py
+++ b/solution.py
@@ -80,6 +80,12 @@
     down_proj,
 ):
     tok_count = queries.shape[0]
+    experts_all = lax.axis_size("expert") * lax.axis_size("dp")
+    own_expert = lax.axis_index("expert") * lax.axis_size("dp") + lax.axis_index("dp")
+    named = expert_ids[:, :, None] == jnp.arange(experts_all, dtype=jnp.int32)[None, None, :]
+    spread = jnp.sum(jnp.where(named, route_weights[:, :, None], 0.0), axis=1)
+    spread = lax.all_gather(spread, ("dp", "expert"), axis=0, tiled=True)
+    own_weight = lax.dynamic_slice_in_dim(spread, own_expert, 1, axis=1)
     heads = beta.shape[1]
     head_dim = norm_gain.shape[0]
     requests = lengths.shape[1]
@@ -89,7 +95,8 @@
     query_n = unit_rows(queries.astype(jnp.float32).reshape(layout)) * head_dim ** (-0.5)
     key_n = unit_rows(keys_in.astype(jnp.float32).reshape(layout))
     value_f = values_in.astype(jnp.float32).reshape(layout)
-    ends = jnp.cumsum(lengths[0])
+    upto = jnp.arange(requests)[:, None] >= jnp.arange(requests)[None, :]
+    ends = jnp.sum(jnp.where(upto, lengths[0][None, :], 0), axis=1)
     places = jnp.arange(tok_count, dtype=jnp.int32)
     request = jnp.sum((places[:, None] >= ends[None, :]).astype(jnp.int32), axis=1)
     member = (request[:, None] == jnp.arange(requests, dtype=jnp.int32)[None, :]).astype(
@@ -125,51 +132,13 @@
     routed = (
         stream * lax.rsqrt(jnp.mean(stream * stream, axis=-1, keepdims=True) + epsilon) * post_gain
     ).astype(jnp.bfloat16)
-    expert_axis = lax.axis_size("expert")
-    data_axis = lax.axis_size("dp")
-    experts_all = expert_axis * data_axis
-    top = expert_ids.shape[1]
-    capacity = min(tok_local, max(2, 5 * tok_local * top // (4 * experts_all)))
-    slots = experts_all * capacity
-    width = routed.shape[1]
-    flat_ids = expert_ids.reshape(-1)
-    chosen = (flat_ids[:, None] == jnp.arange(experts_all, dtype=jnp.int32)[None, :]).astype(
-        jnp.int32
-    )
-    rank = jnp.sum(chosen * (jnp.cumsum(chosen, axis=0) - 1), axis=1)
-    slot_of = flat_ids * capacity + rank
-    picks = (slot_of[None, :] == jnp.arange(slots, dtype=jnp.int32)[:, None]).reshape(
-        slots, tok_local, top
-    )
-    picks = jnp.any(picks, axis=2).astype(jnp.bfloat16)
-    outgoing = jnp.dot(picks, routed, preferred_element_type=jnp.float32).astype(jnp.bfloat16)
-    outgoing = outgoing.reshape(expert_axis, data_axis, capacity, width)
-    arrived = lax.all_to_all(
-        lax.all_to_all(outgoing, "expert", split_axis=0, concat_axis=0, tiled=True),
-        "dp",
-        split_axis=1,
-        concat_axis=1,
-        tiled=True,
-    )
-    shape = arrived.shape
-    flat = arrived.reshape(-1, shape[-1])
-    both = jnp.dot(flat, gate_up[0], preferred_element_type=jnp.float32)
+    rows = lax.all_gather(routed, ("dp", "expert"), axis=0, tiled=True)
+    both = jnp.dot(rows, gate_up[0], preferred_element_type=jnp.float32)
     hidden_width = down_proj.shape[1]
     hidden = (jax.nn.silu(both[:, :hidden_width]) * both[:, hidden_width:]).astype(jnp.bfloat16)
-    result = jnp.dot(hidden, down_proj[0], preferred_element_type=jnp.float32).astype(jnp.bfloat16)
-    returned = lax.all_to_all(
-        lax.all_to_all(result.reshape(shape), "expert", split_axis=0, concat_axis=0, tiled=True),
-        "dp",
-        split_axis=1,
-        concat_axis=1,
-        tiled=True,
-    )
-    gathered = jnp.take(returned.reshape(slots, width), slot_of, axis=0).reshape(
-        tok_local, top, width
-    )
-    moe_out = jnp.sum(gathered.astype(jnp.float32) * route_weights[:, :, None], axis=1).astype(
-        jnp.bfloat16
-    )
+    result = jnp.dot(hidden, down_proj[0], preferred_element_type=jnp.float32)
+    share = (result * own_weight).astype(jnp.bfloat16)
+    moe_out = lax.psum_scatter(share, ("dp", "expert"), scatter_dimension=0, tiled=True)
     return (moe_out, attn_out, new_states)
 
 

time: 538 us -> 500 us (0.929); the launches traced: 528 us -> 498 us
  waiting for transfers between devices: 105 us -> 259 us
  blocking collectives: 194 us -> 70.2 us
  local copies, waits for them, and re-layouts: 83.1 us -> 33.6 us
  other arithmetic: 19.3 us -> 11.7 us
    all_to_all x3 -> x0, blocking collectives: 194 us -> none  [the longest x1 76.5 us: on_device(): lax.all_to_all(result.reshape(shape), 'expert', split_axis=0, concat_axis...]
    reduce_scatter x0 -> x1, waiting for transfers between devices: none -> 182 us  [on_device(): lax.psum_scatter(share, ('dp', 'expert'), scatter_dimension=0, tiled=True)]
    all_gather x0 -> x1, blocking collectives: none -> 70.2 us  [on_device(): spread = lax.all_gather(spread, ('dp', 'expert'), axis=0, tiled=True)]
    all_to_all x1 -> x0, waiting for transfers between devices: 37.1 us -> none  [on_device(): lax.all_to_all(lax.all_to_all(result.reshape(shape), 'expert', split_axis...]
    reshape x7 -> x0, local copies, waits for them, and re-layouts: 28 us -> none  [the longest x2 9.71 us: on_device(): outgoing = outgoing.reshape(expert_axis, data_axis, capacity, width)]
    all_to_all x4 -> x0, local copies, waits for them, and re-layouts: 14.9 us -> none  [the longest x1 5.77 us: on_device(): lax.all_to_all(lax.all_to_all(result.reshape(shape), 'expert', split_axis...]
    gather x2 -> x0, local copies, waits for them, and re-layouts: 9.6 us -> none  [on_device(): jnp.take(returned.reshape(slots, width), slot_of, axis=0)]
    all_gather x0 -> x1, waiting for transfers between devices: none -> 6.06 us  [on_device(): rows = lax.all_gather(routed, ('dp', 'expert'), axis=0, tiled=True)]
  transfers between devices with their start and end apart: 2 -> 3, of which waited for: 2 -> 3; matrix products, arithmetic and copies ran while one was open for 1% -> 1% of each run, Pallas kernels for 0% -> 0%
where the time goes in v1:
time: 500 us; the launch traced here: 498 us
  waiting for transfers between devices  259 us (52%)
  matrix products  107 us (21%)
  blocking collectives  70.2 us (14%)
  local copies, waits for them, and re-layouts  33.6 us (7%)
  between operations  14 us (3%)
  other arithmetic  11.7 us (2%)
    reduce_scatter x1, waiting for transfers between devices, on_device(): lax.psum_scatter(share, ('dp', 'expert'), scatter_dimension=0, tiled=True)  182 us
    reduce_scatter x1, waiting for transfers between devices, on_device(): lax.psum_scatter(jnp.dot(normed, out_proj, preferred_element_type=jnp.flo...  71 us
    all_gather x1, blocking collectives, on_device(): spread = lax.all_gather(spread, ('dp', 'expert'), axis=0, tiled=True)  70.2 us
    dot_general x8, matrix products, block_step(): jnp.einsum('hrc,hck,hcv->hrkv', carried, key_h, updates, precision=HIGH)  18.2 us
    dynamic_slice x32, local copies, waits for them, and re-layouts, on_device(): states, mixed = lax.scan(block_step, jnp.swapaxes(cache, 0, 1), inputs)  15.5 us
    dot_general x8, matrix products, block_step(): jnp.einsum('cr,hrcv->hcv', member_b, from_state, precision=HIGH)  10.7 us
    dot_general x8, matrix products, block_step(): recalled = jnp.einsum('cr,hrcv->hcv', member_b, recalled, precision=HIGH)  10.7 us
    dot_general x40, matrix products, block_step(): jnp.einsum('hij,hjk->hik', inverse, identity + powered, precision=HIGH)  10.3 us
  transfers between devices with their start and end apart: 3, of which 3 were waited for; matrix products, arithmetic and copies ran while one was open for 1% of the time, Pallas kernels for 0%

profile of v1, /device:TPU:0, one launch (start us, length us, event | category | flops | bytes accessed | tf_op | source)
XLA Modules:
  0.0 498.4 jit_solution(1248612116858313740)
XLA Ops:
  9.9 1.4 reshape.123
  12.2 1.5 multiply_multiply_fusion
  13.7 1.4 reshape.119
  16.0 1.6 broadcast_multiply_fusion.1
  17.6 2.4 reshape.121
  21.3 111.9 %while.12 = (s32[]{:T(128)}, f32[4,4,128,128]{3,2,1,0:T(8,128)S(1)}, f32[8,64,4,128]{3,1,2,0:T(8,128)}, f32[8,64,4]{1,0,2:T(8,128)S(1)}, f32[8,64,4]{1,2,0:T(4,1...) while((s32[]{:T(128)}, ...), condition=%wide.region_5.6_spmd, body=%wide.region_4.5_spmd.sunk | while | flops 860401152 | bytes 12359501 | solution.py:113
  33.0 2.3 fusion.214
  47.0 2.3 fusion.214
  61.0 2.3 fusion.214
  74.9 2.3 fusion.214
  88.9 2.3 fusion.214
  102.9 2.3 fusion.214
  116.8 2.3 fusion.214
  130.8 2.3 fusion.214
  133.3 1.6 multiply_reduce_fusion
  134.9 2.9 copy.98
  138.5 4.1 convolution_convert_fusion
  142.7 71.0 %reduce-scatter.3.cloned.1.call-done = bf16[64,2048]{1,0:T(8,128)(2,1)} async-done(((bf16[512,2048]{1,0:T(8,128)(2,1)}), bf16[64,2048]{1,0:T(8,128)(2,1)}) %reduce-scatter.3.cloned.1.call-update) | async-done | bytes 262160 | tf_op jit(solution)/shard_map/reduce_scatter | solution.py:124
  216.0 70.2 %all-gather = f32[32,64,32]{1,2,0:T(8,128)S(1)} all-gather(f32[1,64,32]{1,2,0:T(8,128)S(1)} %bitcast.279), channel_id=1, replica_groups=mesh['groups'=1,'expert'=8,'dp'=4] {'dp','expert'}, dimensions={0}, use_global_device_ids=true | all-gather | bytes 270336 | tf_op jit(solution)/shard_map/all_gather | solution.py:87
  287.3 1.9 reshape.125
  290.1 6.1 %all-gather.3.cloned.1.call-done = bf16[2048,2048]{1,0:T(8,128)(2,1)} async-done(((bf16[64,2048]{1,0:T(8,128)(2,1)}), bf16[2048,2048]{1,0:T(8,128)(2,1)}) %all-gather.3.cloned.1.call-update) | async-done | bytes 8388624 | tf_op jit(solution)/shard_map/all_gather | solution.py:135
  296.1 7.6 %fusion.46 = f32[2048,512]{1,0:T(8,128)S(1)} fusion(bf16[2048,2048]{1,0:T(8,128)(2,1)} %all-gather.3.cloned.1.call-done, bf16[1,2048,512]{2,1,0:T(8,128)(2,1)} %param.32), kind=kOutput, calls=%fused_computation.77 | convolution fusion | flops 4294967296 | bytes 14680064 | tf_op jit(solution)/shard_map/dot_general | solution.py:136
  303.8 4.7 multiply_convert_fusion
  309.6 182.3 %reduce-scatter.5.cloned.1.call-done = bf16[64,2048]{1,0:T(8,128)(2,1)} async-done(((bf16[2048,2048]{1,0:T(8,128)(2,1)}), bf16[64,2048]{1,0:T(8,128)(2,1)}) %reduce-scatter.5.cloned.1.call-update) | async-done | bytes 262160 | tf_op jit(solution)/shard_map/reduce_scatter | solution.py:141
  (311 shorter events, 103.6 us)
Async XLA Ops:
  7.2 131.4 %copy-start = (bf16[512,2048]{1,0:T(8,128)(2,1)S(1)}, bf16[512,2048]{1,0:T(8,128)(2,1)}, u32[]{:S(2)}) copy-start(bf16[512,2048]{1,0:T(8,128)(2,1)} %param.27) | copy-start | bytes 6291460
  7.2 206.5 %reduce-scatter.3.cloned.1.call-start = ((), (), s32[]{:S(2)}) async-start(), calls=%async_computation.2 | async-start | bytes 2359296 | tf_op jit(solution)/shard_map/reduce_scatter | solution.py:124
  133.3 4.5 copy-start.5
  142.7 72.3 %copy-start.2 = (f32[2048]{0:T(1024)S(1)}, f32[2048]{0:T(1024)}, u32[]{:S(2)}) copy-start(f32[2048]{0:T(1024)} %param.29) | copy-start | bytes 24580
  142.7 73.2 %copy-start.3 = (f32[64,10]{0,1:T(8,128)S(1)}, f32[64,10]{0,1:T(8,128)}, u32[]{:S(2)}) copy-start(f32[64,10]{0,1:T(8,128)} %param.31) | copy-start | bytes 7684
  142.7 73.3 %copy-start.4 = (s32[64,10]{0,1:T(8,128)S(1)}, s32[64,10]{0,1:T(8,128)}, u32[]{:S(2)}) copy-start(s32[64,10]{0,1:T(8,128)} %param.30) | copy-start | bytes 7684
  142.7 153.4 %all-gather.3.cloned.1.call-start = ((), (), s32[]{:S(2)}) async-start(), calls=%async_computation.3 | async-start | bytes 8650752 | tf_op jit(solution)/shard_map/all_gather | solution.py:135
  215.0 88.8 %copy-start.1 = (bf16[64,2048]{1,0:T(8,128)(2,1)}, bf16[64,2048]{1,0:T(8,128)(2,1)S(1)}, u32[]{:S(2)}) copy-start(bf16[64,2048]{1,0:T(8,128)(2,1)S(1)} %get-tuple-element.126) | copy-start | bytes 786436
  215.8 276.0 %reduce-scatter.5.cloned.1.call-start = ((), (), s32[]{:S(2)}) async-start(), calls=%async_computation.4 | async-start | bytes 8650752 | tf_op jit(solution)/shard_map/reduce_scatter | solution.py:141
  296.1 7.6 %copy-start.6 = (bf16[1,256,2048]{2,1,0:T(8,128)(2,1)S(1)}, bf16[1,256,2048]{2,1,0:T(8,128)(2,1)}, u32[]{:S(2)}) copy-start(bf16[1,256,2048]{2,1,0:T(8,128)(2,1)} %param.33) | copy-start | bytes 3145732
Sparse Core Ops, SparseCore 0:
  142.8 70.8 reduce-scatter.2
  216.7 79.3 all-gather.2
  308.6 183.1 reduce-scatter.4

commit v2 on v1

v2 whole, which is shorter than its diff:
```python
import jax
import jax.numpy as jnp
from jax import lax
from jax.experimental import pallas as pl
from jax.experimental.pallas import tpu as pltpu
from jax.sharding import PartitionSpec as P

HIGH = lax.Precision.HIGHEST
epsilon = 1e-06
block_rows = 64


def dot(a, b, dims=((1,), (0,))):
    return lax.dot_general(a, b, (dims, ((), ())), preferred_element_type=jnp.float32)


def halves(a):
    high = a.astype(jnp.bfloat16)
    return high, (a - high.astype(jnp.float32)).astype(jnp.bfloat16)


def fine_dot(a, b):
    a_high, a_low = halves(a)
    b_high, b_low = halves(b)
    return dot(a_high, b_high) + (dot(a_high, b_low) + dot(a_low, b_high))


def unit_inverse(lower, row, column):
    size = lower.shape[0]

    def same(width):
        shift = width.bit_length() - 1
        return (row >> shift) == (column >> shift)

    width = min(8, size)
    identity = jnp.where(row == column, 1.0, 0.0)
    first = jnp.where(same(width), lower, 0.0)
    second = fine_dot(first, first)
    fourth = fine_dot(second, second)
    inverse = identity - first
    inverse = inverse + fine_dot(inverse, second)
    inverse = inverse + fine_dot(inverse, fourth)
    while width < size:
        between = jnp.where(same(2 * width) & jnp.logical_not(same(width)), lower, 0.0)
        inverse = inverse - fine_dot(inverse, fine_dot(between, inverse))
        width = 2 * width
    return inverse


def mix_kernel(
    queries, keys, values, gates, beta, decay, decay_t, request, request_t, cache, gain,
    normed, new_states, states,
):
    requests, heads, head_dim, _ = cache.shape
    blocks, _, size = request_t.shape
    for h in range(heads):
        for r in range(requests):
            states[h, :, r * head_dim : (r + 1) * head_dim] = cache[r, h]
    row = lax.broadcasted_iota(jnp.int32, (size, size), 0)
    column = lax.broadcasted_iota(jnp.int32, (size, size), 1)

    def step(block, carry):
        rows = pl.ds(pl.multiple_of(block * size, size), size)
        owner = request[rows, :]
        shared = owner == request_t[block]
        inside = shared & (row >= column)
        strict = shared & (row > column)
        inside_f = inside.astype(jnp.float32)
        decay_b = decay[rows, :]
        running = jnp.dot(inside_f, decay_b, precision=HIGH, preferred_element_type=jnp.float32)
        running_t = lax.dot_general(
            decay_t[block], inside_f, (((1,), (1,)), ((), ())),
            precision=HIGH, preferred_element_type=jnp.float32,
        )
        total = jnp.dot(
            shared.astype(jnp.float32), decay_b,
            precision=HIGH, preferred_element_type=jnp.float32,
        )
        growth_all = jnp.exp(running)
        carried_all = jnp.exp(jnp.minimum(total - running, 0.0))
        beta_b = beta[rows, :]
        for h in range(heads):
            lanes = slice(h * head_dim, (h + 1) * head_dim)
            query, key = queries[rows, lanes], keys[rows, lanes]
            query_f, key_f = query.astype(jnp.float32), key.astype(jnp.float32)
            query_s = lax.rsqrt(jnp.sum(query_f * query_f, axis=1, keepdims=True) + epsilon)
            query_s = query_s * head_dim ** (-0.5)
            key_s = lax.rsqrt(jnp.sum(key_f * key_f, axis=1, keepdims=True) + epsilon)
            growth = growth_all[:, h : h + 1]
            write = beta_b[:, h : h + 1] * key_s
            gaps = running[:, h : h + 1] - running_t[h : h + 1, :]
            decays = jnp.where(inside, jnp.exp(jnp.minimum(gaps, 0.0)), 0.0)
            both = jnp.concatenate([key, query], axis=0)
            dots = dot(both, key, ((1,), (1,)))
            lower = jnp.where(strict, decays * dots[:size] * (write * key_s), 0.0)
            inverse = unit_inverse(lower, row, column)
            state = states[h]
            high, low = halves(state)
            recalled_all = dot(both, high) + dot(both, low)
            recalled = jnp.zeros((size, head_dim), jnp.float32)
            asked = jnp.zeros((size, head_dim), jnp.float32)
            for r in range(requests):
                part = recalled_all[:, r * head_dim : (r + 1) * head_dim]
                recalled = jnp.where(owner == r, part[:size], recalled)
                asked = jnp.where(owner == r, part[size:], asked)
            value = values[rows, lanes].astype(jnp.float32)
            updates = fine_dot(inverse, write * (value - growth * key_s * recalled))
            mixed = growth * asked + dot(
                (decays * dots[size:]).astype(jnp.bfloat16), updates.astype(jnp.bfloat16)
            )
            mixed = mixed * query_s
            kept = carried_all[:, h : h + 1] * updates
            spread = jnp.concatenate(
                [jnp.where(owner == r, kept, 0.0) for r in range(requests)], axis=1
            )
            high, low = halves(spread)
            fresh = dot(key, high, ((0,), (0,))) + dot(key, low, ((0,), (0,)))
            for r in range(requests):
                part = slice(r * head_dim, (r + 1) * head_dim)
                span = jnp.sum(
                    jnp.where(owner == r, decay_b[:, h : h + 1], 0.0), axis=0, keepdims=True
                )
                states[h, :, part] = jnp.exp(span) * state[:, part] + fresh[:, part]
            gate = gates[rows, lanes].astype(jnp.float32)
            scale = lax.rsqrt(jnp.mean(mixed * mixed, axis=1, keepdims=True) + epsilon)
            normed[rows, lanes] = (mixed * scale * gain[...] * jax.nn.silu(gate)).astype(
                jnp.bfloat16
            )
        return carry

    lax.fori_loop(0, blocks, step, 0)
    for h in range(heads):
        for r in range(requests):
            new_states[r, h] = states[h, :, r * head_dim : (r + 1) * head_dim]


def on_device(
    queries,
    keys_in,
    values_in,
    gate_in,
    beta,
    decay,
    lengths,
    cache,
    norm_gain,
    out_proj,
    residual,
    post_gain,
    expert_ids,
    route_weights,
    gate_up,
    down_proj,
):
    tok_count = queries.shape[0]
    experts_all = lax.axis_size("expert") * lax.axis_size("dp")
    own_expert = lax.axis_index("expert") * lax.axis_size("dp") + lax.axis_index("dp")
    named = expert_ids[:, :, None] == jnp.arange(experts_all, dtype=jnp.int32)[None, None, :]
    spread = jnp.sum(jnp.where(named, route_weights[:, :, None], 0.0), axis=1)
    spread = lax.all_gather(spread, ("dp", "expert"), axis=0, tiled=True)
    own_weight = lax.dynamic_slice_in_dim(spread, own_expert, 1, axis=1)
    heads = beta.shape[1]
    head_dim = norm_gain.shape[0]
    requests = lengths.shape[1]
    block = min(block_rows, tok_count)
    blocks = tok_count // block
    upto = jnp.arange(requests)[:, None] >= jnp.arange(requests)[None, :]
    ends = jnp.sum(jnp.where(upto, lengths[0][None, :], 0), axis=1)
    places = jnp.arange(tok_count, dtype=jnp.int32)
    request = jnp.sum((places[:, None] >= ends[None, :]).astype(jnp.int32), axis=1)
    normed, new_states = pl.pallas_call(
        mix_kernel,
        out_shape=(
            jax.ShapeDtypeStruct(queries.shape, jnp.bfloat16),
            jax.ShapeDtypeStruct(cache.shape, jnp.float32),
        ),
        in_specs=[pl.BlockSpec(memory_space=pltpu.VMEM)] * 11,
        out_specs=[pl.BlockSpec(memory_space=pltpu.VMEM)] * 2,
        scratch_shapes=[pltpu.VMEM((heads, head_dim, requests * head_dim), jnp.float32)],
        compiler_params=pltpu.CompilerParams(vmem_limit_bytes=40 * 1024 * 1024),
    )(
        queries,
        keys_in,
        values_in,
        gate_in,
        beta,
        decay,
        jnp.swapaxes(decay.reshape(blocks, block, heads), 1, 2),
        request[:, None],
        request.reshape(blocks, 1, block),
        cache,
        norm_gain[None, :],
    )
    tok_local = residual.shape[0]
    attn = lax.psum_scatter(
        jnp.dot(normed, out_proj, preferred_element_type=jnp.float32).astype(jnp.bfloat16),
        "expert",
        scatter_dimension=0,
        tiled=True,
    ).astype(jnp.float32)
    attn_out = (residual.astype(jnp.float32) + attn).astype(jnp.bfloat16)
    stream = attn_out.astype(jnp.float32)
    routed = (
        stream * lax.rsqrt(jnp.mean(stream * stream, axis=-1, keepdims=True) + epsilon) * post_gain
    ).astype(jnp.bfloat16)
    rows = lax.all_gather(routed, ("dp", "expert"), axis=0, tiled=True)
    both = jnp.dot(rows, gate_up[0], preferred_element_type=jnp.float32)
    hidden_width = down_proj.shape[1]
    hidden = (jax.nn.silu(both[:, :hidden_width]) * both[:, hidden_width:]).astype(jnp.bfloat16)
    result = jnp.dot(hidden, down_proj[0], preferred_element_type=jnp.float32)
    share = (result * own_weight).astype(jnp.bfloat16)
    share = lax.psum_scatter(share, "dp", scatter_dimension=0, tiled=True)
    moe_out = lax.psum_scatter(share, "expert", scatter_dimension=0, tiled=True)
    return (moe_out, attn_out, new_states)


def solution(mesh):
    return jax.shard_map(
        on_device,
        mesh=mesh,
        in_specs=(
            P(("groups", "dp"), "expert"),
            P(("groups", "dp"), "expert"),
            P(("groups", "dp"), "expert"),
            P(("groups", "dp"), "expert"),
            P(("groups", "dp"), "expert"),
            P(("groups", "dp"), "expert"),
            P(("groups", "dp"), None),
            P(("groups", "dp"), "expert", None, None),
            P(),
            P("expert", None),
            P(("groups", "dp", "expert"), None),
            P(),
            P(("groups", "dp", "expert"), None),
            P(("groups", "dp", "expert"), None),
            P(("expert", "dp"), None, None),
            P(("expert", "dp"), None, None),
        ),
        out_specs=(
            P(("groups", "dp", "expert"), None),
            P(("groups", "dp", "expert"), None),
            P(("groups", "dp"), "expert", None, None),
        ),
        check_vma=False,
    )
```

time: 500 us -> 395 us (0.79)
  matrix products: 107 us -> 14.9 us
  Pallas kernels: 0 us -> 60.4 us
  waiting for transfers between devices: 259 us -> 223 us
  local copies, waits for them, and re-layouts: 33.6 us -> 9.41 us
  other arithmetic: 11.7 us -> 2.88 us
    dot_general x176 -> x0, matrix products: 91 us -> none  [the longest x8 18.2 us: block_step(): jnp.einsum('hrc,hck,hcv->hrkv', carried, key_h, updates, precision=HIGH)]
    pallas_call x0 -> x1, Pallas kernels: none -> 60.4 us  [on_device(): pl.pallas_call(mix_kernel, out_shape=(jax.ShapeDtypeStruct(queries.shape,...]
    reduce_scatter x1 -> x2, waiting for transfers between devices: 182 us -> 143 us  [the longest x1 72.1 us: on_device(): moe_out = lax.psum_scatter(share, 'expert', scatter_dimension=0, tiled=True)]
    dynamic_slice x32 -> x0, local copies, waits for them, and re-layouts: 15.5 us -> none  [on_device(): states, mixed = lax.scan(block_step, jnp.swapaxes(cache, 0, 1), inputs)]
    reshape x4 -> x1, local copies, waits for them, and re-layouts: 5.91 us -> 0.09 us  [on_device(): request.reshape(blocks, 1, block)]
  transfers between devices with their start and end apart: 3 -> 4, of which waited for: 3 -> 4; matrix products, arithmetic and copies ran while one was open for 1% -> 0% of each run, Pallas kernels for 0% -> 0%
where the time goes in v2:
time: 395 us
  waiting for transfers between devices  223 us (56%)
  blocking collectives  70.1 us (18%)
  Pallas kernels  60.4 us (15%)
  matrix products  14.9 us (4%)
  between operations  13.9 us (4%)
  local copies, waits for them, and re-layouts  9.41 us (2%)
    reduce_scatter x1, waiting for transfers between devices, on_device(): moe_out = lax.psum_scatter(share, 'expert', scatter_dimension=0, tiled=True)  72.1 us
    reduce_scatter x1, waiting for transfers between devices, on_device(): share = lax.psum_scatter(share, 'dp', scatter_dimension=0, tiled=True)  70.6 us
    reduce_scatter x1, waiting for transfers between devices, on_device(): lax.psum_scatter(jnp.dot(normed, out_proj, preferred_element_type=jnp.flo...  70.4 us
    all_gather x1, blocking collectives, on_device(): spread = lax.all_gather(spread, ('dp', 'expert'), axis=0, tiled=True)  70.1 us
    pallas_call x1, Pallas kernels, on_device(): pl.pallas_call(mix_kernel, out_shape=(jax.ShapeDtypeStruct(queries.shape,...  60.4 us
    all_gather x1, waiting for transfers between devices, on_device(): rows = lax.all_gather(routed, ('dp', 'expert'), axis=0, tiled=True)  9.77 us
    unnamed x29, local copies, waits for them, and re-layouts  7.94 us
  transfers between devices with their start and end apart: 4, of which 4 were waited for; matrix products, arithmetic and copies ran while one was open for 0% of the time, Pallas kernels for 0%

profile of v2, /device:TPU:0, one launch (start us, length us, event | category | flops | bytes accessed | tf_op | source)
XLA Modules:
  0.0 394.6 jit_solution(9130868056319130565)
XLA Ops:
  7.2 0.9 reshape.24
  8.1 0.8 copy.44.decay
  9.0 0.8 select_reduce_fusion.1
  9.9 0.1 copy.45.request
  10.1 0.8 copy.43.beta
  11.0 1.2 copy-done.1
  12.2 1.0 copy-done.2
  13.2 1.0 copy-done.3
  14.3 1.0 copy-done.4
  15.3 1.0 copy-done.5
  16.3 0.7 copy-done.6
  17.0 60.4 %shard_map.175 = (bf16[512,512]{1,0:T(8,128)(2,1)S(1)}, f32[4,4,128,128]{3,2,1,0:T(8,128)}) custom-call(bf16[512,512]{1,0:T(8,128)(2,1)S(1)} %copy-done.2, bf16[512,512]{1,0:T(8,128)(2,1)S(1)} %copy-done.3, bf16[512,512]{1,0:T(8,128)(2,1)S(1)} %copy-done.4, bf16[512,512]{1,0:T(8,128)(2,1)S(1)} %copy-done.5, f32[512,4]{1,0:T(8,128)S(1)} %copy.43.beta, ...), custom_call_target="tpu_custom_call" | custom-call | tf_op jit(solution)/shard_map/pallas_call | solution.py:171
  77.4 2.6 convolution_convert_fusion
  80.1 70.4 %reduce-scatter.4.cloned.1.call-done = bf16[64,2048]{1,0:T(8,128)(2,1)} async-done(((bf16[512,2048]{1,0:T(8,128)(2,1)}), bf16[64,2048]{1,0:T(8,128)(2,1)}) %reduce-scatter.4.cloned.1.call-update) | async-done | bytes 262160 | tf_op jit(solution)/shard_map/reduce_scatter | solution.py:195
  150.5 1.1 fusion.6
  151.7 0.8 fusion.8
  152.6 70.1 %all-gather = f32[32,64,32]{1,2,0:T(8,128)S(1)} all-gather(f32[1,64,32]{1,2,0:T(8,128)S(1)} %bitcast.23), channel_id=1, replica_groups=mesh['groups'=1,'expert'=8,'dp'=4] {'dp','expert'}, dimensions={0}, use_global_device_ids=true | all-gather | bytes 270336 | tf_op jit(solution)/shard_map/all_gather | solution.py:160
  222.7 0.3 copy.46
  223.0 0.2 reshape.27
  223.3 9.8 %all-gather.3.cloned.1.call-done = bf16[2048,2048]{1,0:T(8,128)(2,1)} async-done(((bf16[64,2048]{1,0:T(8,128)(2,1)}), bf16[2048,2048]{1,0:T(8,128)(2,1)}) %all-gather.3.cloned.1.call-update) | async-done | bytes 8388624 | tf_op jit(solution)/shard_map/all_gather | solution.py:206
  233.0 7.5 %fusion.1 = f32[2048,512]{1,0:T(8,128)S(1)} fusion(bf16[2048,2048]{1,0:T(8,128)(2,1)} %all-gather.3.cloned.1.call-done, bf16[1,2048,512]{2,1,0:T(8,128)(2,1)} %param.30), kind=kOutput, calls=%fused_computation.4 | convolution fusion | flops 4294967296 | bytes 14680064 | tf_op jit(solution)/shard_map/dot_general | solution.py:207
  240.6 4.7 %multiply_convert_fusion = bf16[2048,2048]{1,0:T(8,128)(2,1)} fusion(f32[2048]{0:T(1024)S(1)} %bitcast.25, f32[2048,512]{1,0:T(8,128)S(1)} %fusion.1, bf16[1,256,2048]{2,1,0:T(8,128)(2,1)S(1)} %copy-done.12), kind=kOutput, calls=%fused_computation | convolution fusion | flops 2159017984 | bytes 13639680 | tf_op jit(solution)/shard_map/dot_general | solution.py:210
  245.4 70.6 %reduce-scatter.6.cloned.1.call-done = bf16[512,2048]{1,0:T(8,128)(2,1)} async-done(((bf16[2048,2048]{1,0:T(8,128)(2,1)}), bf16[512,2048]{1,0:T(8,128)(2,1)}) %reduce-scatter.6.cloned.1.call-update) | async-done | bytes 2097168 | tf_op jit(solution)/shard_map/reduce_scatter | solution.py:212
  316.0 72.1 %reduce-scatter.8.cloned.1.call-done = bf16[64,2048]{1,0:T(8,128)(2,1)} async-done(((bf16[512,2048]{1,0:T(8,128)(2,1)}), bf16[64,2048]{1,0:T(8,128)(2,1)}) %reduce-scatter.8.cloned.1.call-update) | async-done | bytes 262160 | tf_op jit(solution)/shard_map/reduce_scatter | solution.py:213
  (34 shorter events, 0.5 us)
Async XLA Ops:
  7.2 70.2 %copy-start = (bf16[512,2048]{1,0:T(8,128)(2,1)S(1)}, bf16[512,2048]{1,0:T(8,128)(2,1)}, u32[]{:S(2)}) copy-start(bf16[512,2048]{1,0:T(8,128)(2,1)} %param.25) | copy-start | bytes 6291460
  7.2 143.3 %reduce-scatter.4.cloned.1.call-start = ((), (), s32[]{:S(2)}) async-start(), calls=%async_computation.3 | async-start | bytes 2359296 | tf_op jit(solution)/shard_map/reduce_scatter | solution.py:195
  10.9 1.2 copy-start.1
  12.2 1.0 copy-start.2
  13.2 1.0 copy-start.3
  14.3 1.0 copy-start.4
  15.3 1.0 copy-start.5
  16.3 0.7 copy-start.6
  80.0 70.5 %copy-start.8 = (bf16[64,2048]{1,0:T(8,128)(2,1)S(1)}, bf16[64,2048]{1,0:T(8,128)(2,1)}, u32[]{:S(2)}) copy-start(bf16[64,2048]{1,0:T(8,128)(2,1)} %param.26) | copy-start | bytes 786436
  80.0 71.7 %copy-start.9 = (f32[2048]{0:T(1024)S(1)}, f32[2048]{0:T(1024)}, u32[]{:S(2)}) copy-start(f32[2048]{0:T(1024)} %param.27) | copy-start | bytes 24580
  80.0 72.6 %copy-start.10 = (f32[64,10]{0,1:T(8,128)S(1)}, f32[64,10]{0,1:T(8,128)}, u32[]{:S(2)}) copy-start(f32[64,10]{0,1:T(8,128)} %param.29) | copy-start | bytes 7684
  80.0 72.6 %copy-start.11 = (s32[64,10]{0,1:T(8,128)S(1)}, s32[64,10]{0,1:T(8,128)}, u32[]{:S(2)}) copy-start(s32[64,10]{0,1:T(8,128)} %param.28) | copy-start | bytes 7684
  80.1 153.0 %all-gather.3.cloned.1.call-start = ((), (), s32[]{:S(2)}) async-start(), calls=%async_computation.4 | async-start | bytes 8650752 | tf_op jit(solution)/shard_map/all_gather | solution.py:206
  151.6 88.9 %copy-start.7 = (bf16[64,2048]{1,0:T(8,128)(2,1)}, bf16[64,2048]{1,0:T(8,128)(2,1)S(1)}, u32[]{:S(2)}) copy-start(bf16[64,2048]{1,0:T(8,128)(2,1)S(1)} %get-tuple-element.8) | copy-start | bytes 786436
  152.5 163.4 %reduce-scatter.6.cloned.1.call-start = ((), (), s32[]{:S(2)}) async-start(), calls=%async_computation.5 | async-start | bytes 10485760 | tf_op jit(solution)/shard_map/reduce_scatter | solution.py:212
  223.2 17.3 %copy-start.12 = (bf16[1,256,2048]{2,1,0:T(8,128)(2,1)S(1)}, bf16[1,256,2048]{2,1,0:T(8,128)(2,1)}, u32[]{:S(2)}) copy-start(bf16[1,256,2048]{2,1,0:T(8,128)(2,1)} %param.31) | copy-start | bytes 3145732
  245.3 142.8 %reduce-scatter.8.cloned.1.call-start = ((), (), s32[]{:S(2)}) async-start(), calls=%async_computation.6 | async-start | bytes 2359296 | tf_op jit(solution)/shard_map/reduce_scatter | solution.py:213
Sparse Core Ops, SparseCore 0:
  80.2 70.2 reduce-scatter.3
  154.0 78.9 all-gather.2
  245.5 70.4 reduce-scatter.5
  320.3 67.7 reduce-scatter.7
